TPU v7x, 128 devices: a whole 4x4x4 slice. The times are simulated.
128 devices in a mesh: dp: 8 (over x, core), tensor: 16 (over y, z).
Axes of the slice: x: 4, y: 4, z: 4, core: 2. Of those that a mesh axis runs over, the one named last changes fastest.
Arguments:
- stream: bfloat16 [16, 4, 8192], P('dp', None, 'tensor'), may hold values from -6 to 6
- norm_gain: bfloat16 [8192], P('tensor'), may hold values from 0.5 to 1.5
- w_q: bfloat16 [8192, 64, 128], P(None, 'tensor'), may hold values from -0.0625 to 0.0625
- w_kv: bfloat16 [8192, 16, 256], P(None, 'tensor'), as said below
- w_o: bfloat16 [64, 128, 8192], P('tensor'), may hold values from -0.0625 to 0.0625
- prefix_kv: bfloat16 [4, 2048, 16, 256], P(None, 'dp', 'tensor'), may hold values from -620 to 620, as said below
- prompt_len: int32 [4], replicated, may hold values from 512 to 2048, as said below
- suffix_kv: bfloat16 [16, 4, 256, 16, 256], P('dp', None, None, 'tensor'), may hold values from -6 to 6, as said below
- suffix_len: int32 [16, 4], replicated, may hold values from 0 to 255, as said below
- log_weight: float32 [16, 4], P('dp'), may hold values from -12 to 412
- potential: bfloat16 [8192], P('tensor'), may hold values from -0.0625 to 0.0625
- anc_group: int32 [16, 4, 1], replicated, may hold values from 0 to 7; in each aligned block of 8 rows (0 to 7, 8 to 15, ..., all dimensions but the last counted through in order) at most 2 rows name the same one
- anc_member: int32 [16, 4], replicated, may hold values from 0 to 1
Outputs:
- mixed: bfloat16 [16, 4, 8192], P('dp', None, 'tensor')
- normalized: float32 [16, 4], P('dp')
- new_suffix: bfloat16 [16, 4, 256, 16, 256], P('dp', None, None, 'tensor')
Inputs may be any that keep to these rules, and one draw needn't show every extreme that they name: Ancestor particle of particle p in prompt q is 2 * anc_group[p, q, 0] + anc_member[p, q]. Among the rows of one block (8 rows in order, particle-major), at most 2 name one block, and some block is named by exactly 2 of them. `prompt_len`: some prompt has all 2048 positions. `suffix_len`: some particle has 255. `w_kv`: copies 2 k and 2 k + 1 along the middle dimension are equal; both hold key head k. `prefix_kv`: copies 2 k and 2 k + 1 along the third dimension are equal; both hold key head k. `suffix_kv`: copies 2 k and 2 k + 1 along the fourth dimension are equal; both hold key head k.
All inputs are finite; a program needn't handle non-finite values.
Results may differ from a plain program's by a relative error of at most 0.011.
Values may be sent and summed in bfloat16 or wider, within the bound.
A program may use at most 128 MiB of HBM per device.

v0:
```python
import jax
import jax.numpy as jnp
from jax import lax
from jax.sharding import PartitionSpec as P


def per_device(
    stream,
    norm_gain,
    w_q,
    w_kv,
    w_o,
    prefix_kv,
    prompt_len,
    suffix_kv,
    suffix_len,
    log_weight,
    potential,
    anc_group,
    anc_member,
):
    slot_count = stream.shape[0]
    prompt_count = stream.shape[1]
    model_width = w_q.shape[0]
    local_heads = w_q.shape[1]
    head_dim = w_q.shape[2]
    copy_count = w_kv.shape[1]
    per_copy = local_heads // copy_count
    spread = suffix_kv.shape[2]
    rank_dp = lax.axis_index("dp")
    full_x, full_gain = (
        lax.all_gather(stream, "tensor", axis=2, tiled=True),
        lax.all_gather(norm_gain, "tensor", axis=0, tiled=True),
    )
    xfloat = full_x.astype(jnp.float32)
    meansq = jnp.mean(xfloat * xfloat, axis=-1, keepdims=True)
    normed = (xfloat * lax.rsqrt(meansq + 1e-05) * full_gain.astype(jnp.float32)).astype(
        jnp.bfloat16
    )
    normed = normed.reshape(slot_count * prompt_count, model_width)
    queries = (
        jnp.dot(normed, w_q.reshape(model_width, -1), preferred_element_type=jnp.float32)
        * head_dim ** (-0.5)
    ).astype(jnp.bfloat16)
    queries = queries.reshape(slot_count, prompt_count, copy_count, per_copy, head_dim)
    fresh = jnp.dot(
        normed, w_kv.reshape(model_width, -1), preferred_element_type=jnp.float32
    ).astype(jnp.bfloat16)
    fresh = fresh.reshape(slot_count, prompt_count, copy_count, 2 * head_dim)
    own_len = lax.dynamic_slice_in_dim(suffix_len, rank_dp * slot_count, slot_count, 0)
    places = jnp.arange(spread, dtype=jnp.int32)
    landing = places[None, None, :] == own_len[:, :, None]
    appended = jnp.where(landing[:, :, :, None, None], fresh[:, :, None], suffix_kv)
    suf_scores = jnp.einsum(
        "sqcgd,sqlcd->sqcgl", queries, appended[..., :head_dim], preferred_element_type=jnp.float32
    )
    suf_mask = places[None, None, :] <= own_len[:, :, None]
    suf_scores = jnp.where(suf_mask[:, :, None, None, :], suf_scores, -jnp.inf)
    suf_top = jnp.max(suf_scores, axis=-1)
    prefix_all = lax.all_gather(prefix_kv, "dp", axis=1, tiled=True)
    pre_mask = jnp.arange(prefix_all.shape[1], dtype=jnp.int32)[None, :] < prompt_len[:, None]
    pre_scores = jnp.einsum(
        "sqcgd,qlcd->sqcgl", queries, prefix_all[..., :head_dim], preferred_element_type=jnp.float32
    )
    pre_scores = jnp.where(pre_mask[None, :, None, None, :], pre_scores, -jnp.inf)
    highest = jnp.maximum(jnp.max(pre_scores, axis=-1), suf_top)
    pre_exp = jnp.exp(pre_scores - highest[..., None])
    suf_exp = jnp.exp(suf_scores - highest[..., None])
    totals = jnp.sum(pre_exp, axis=-1) + jnp.sum(suf_exp, axis=-1)
    pre_weights = (pre_exp / totals[..., None]).astype(jnp.bfloat16)
    suf_weights = (suf_exp / totals[..., None]).astype(jnp.bfloat16)
    attended = jnp.einsum(
        "sqcgl,qlcd->sqcgd",
        pre_weights,
        prefix_all[..., head_dim:],
        preferred_element_type=jnp.float32,
    )
    attended = attended + jnp.einsum(
        "sqcgl,sqlcd->sqcgd",
        suf_weights,
        appended[..., head_dim:],
        preferred_element_type=jnp.float32,
    )
    attended = attended.astype(jnp.bfloat16).reshape(slot_count * prompt_count, -1)
    projected = jnp.dot(attended, w_o.reshape(-1, model_width), preferred_element_type=jnp.float32)
    projected = projected.reshape(slot_count, prompt_count, model_width)
    shared = lax.psum_scatter(projected, "tensor", scatter_dimension=2, tiled=True)
    mixed = (stream.astype(jnp.float32) + shared).astype(jnp.bfloat16)
    partial_dot = jnp.sum(mixed.astype(jnp.float32) * potential.astype(jnp.float32), axis=-1)
    updated = log_weight + lax.psum(partial_dot, "tensor")
    every_weight = lax.all_gather(updated, "dp", axis=0, tiled=True)
    whole_best = jnp.max(every_weight, axis=0)
    log_total = whole_best + jnp.log(jnp.sum(jnp.exp(every_weight - whole_best[None, :]), axis=0))
    normalized = updated - log_total[None, :]
    groups = anc_group[:, :, 0]
    prompt_index = jnp.arange(prompt_count, dtype=jnp.int32)
    ancestor = groups * slot_count + anc_member
    own_ancestor = lax.dynamic_slice_in_dim(ancestor, rank_dp * slot_count, slot_count, 0)
    piece = lax.all_gather(appended, "dp", axis=0, tiled=True)
    row_count = piece.shape[0]
    inside = (own_ancestor >= 0) & (own_ancestor < row_count)
    picked = piece[jnp.clip(own_ancestor, 0, row_count - 1), prompt_index[None, :]]
    new_suffix = jnp.where(inside[:, :, None, None, None], picked, jnp.zeros_like(appended))
    return (mixed, normalized, new_suffix)


def solution(mesh):
    placed = (
        P("dp", None, "tensor"),
        P("tensor"),
        P(None, "tensor", None),
        P(None, "tensor", None),
        P("tensor", None, None),
        P(None, "dp", "tensor", None),
        P(),
        P("dp", None, None, "tensor", None),
        P(),
        P("dp", None),
        P("tensor"),
        P(),
        P(),
    )
    return jax.shard_map(
        per_device,
        mesh=mesh,
        in_specs=placed,
        out_specs=(P("dp", None, "tensor"), P("dp", None), P("dp", None, None, "tensor", None)),
        check_vma=False,
    )
```

profile of v0, /device:TPU:1, one launch (start us, length us, event | category | flops | bytes accessed | tf_op | source)
XLA Modules:
  0.0 234.9 jit_solution(9065694971450868889)
XLA Ops:
  7.2 0.7 all-gather.5.cloned.1.call-update
  7.9 0.7 broadcast_multiply_fusion
  8.6 0.7 add.55
  9.3 0.8 fusion.33
  10.2 0.7 reshape.178
  10.9 20.9 %all-gather = bf16[16,1,512]{2,1,0:T(2,128)(2,1)S(1)} all-gather(bf16[1,1,512]{2,1,0:T(2,128)(2,1)S(1)} %reshape.178), channel_id=1, replica_groups=mesh['dp'=8,'tensor'=16] {'tensor'}, dimensions={0}, use_global_device_ids=true | all-gather | bytes 17408 | tf_op jit(solution)/shard_map/all_gather | solution.py:33
  31.8 18.7 %all_gather.15 = bf16[2,4,8192]{2,1,0:T(4,128)(2,1)S(1)} all-gather(bf16[2,4,512]{2,1,0:T(4,128)(2,1)} %param.13), channel_id=1, replica_groups=mesh['dp'=8,'tensor'=16] {'tensor'}, dimensions={2}, use_global_device_ids=true | all-gather | bytes 139264 | tf_op jit(solution)/shard_map/all_gather | solution.py:32
  50.6 0.2 fusion.21
  50.7 0.1 fusion.23
  50.9 2.8 %fusion.17 = bf16[8,256]{1,0:T(8,128)(2,1)S(1)} fusion(bf16[8,8192]{1,0:T(8,128)(2,1)S(1)} %reshape.154, bf16[8192,1,256]{2,0,1:T(8,128)(2,1)} %param.16), kind=kOutput, calls=%fused_computation.19 | convolution fusion | flops 33556480 | bytes 4329472 | tf_op jit(solution)/shard_map/dot_general | solution.py:46
  53.8 4.7 %fusion.13 = bf16[8,512]{1,0:T(8,128)(2,1)S(1)} fusion(bf16[8,8192]{1,0:T(8,128)(2,1)S(1)} %reshape.154, bf16[1024,8,4,128]{3,2,1,0:T(4,128)(2,1)} %bitcast.94), kind=kOutput, calls=%fused_computation.17 | convolution fusion | flops 67117056 | bytes 8527872 | tf_op jit(solution)/shard_map/dot_general | solution.py:42
  58.6 0.4 bitcast_select_fusion
  59.0 0.3 fusion.34
  59.5 2.3 fusion.35
  61.8 0.2 fusion.27
  62.0 0.2 fusion.24
  62.3 2.1 fusion.8
  64.4 0.2 fusion.16
  64.6 4.6 %fusion.29 = f32[2,4,8192]{2,1,0:T(4,128)S(1)} fusion(bf16[512,8192,1]{1,0,2:T(8,128)(2,1)} %bitcast.95, bf16[2,4,512]{2,0,1:T(2,128)(2,1)S(1)} %dot_general.44), kind=kOutput, calls=%fused_computation.42 | convolution fusion | flops 67108864 | bytes 8658944 | tf_op jit(solution)/shard_map/dot_general | solution.py:85
  69.2 7.8 %copy.72 = f32[2,4,8192]{1,0,2:T(2,128)} copy(f32[2,4,8192]{2,1,0:T(4,128)S(1)} %fusion.29) | data formatting | bytes 524288
  77.1 8.8 %reshape.186 = f32[8192,8]{1,0:T(8,128)} reshape(f32[8192,2,4]{2,1,0:T(2,128)} %bitcast.93) | data formatting | bytes 524288
  86.0 1.2 fusion.40
  87.5 0.1 copy.63
  87.6 82.2 %reduce-scatter.4.cloned.1.call-done = f32[512,8]{1,0:T(8,128)} async-done(((f32[8192,8]{1,0:T(8,128)}), f32[512,8]{1,0:T(8,128)}) %reduce-scatter.4.cloned.1.call-update) | async-done | bytes 16400
  169.8 1.3 reshape.187
  171.1 0.2 copy.73
  171.3 0.6 multiply_reduce_fusion
  171.9 30.9 %psum.7 = f32[2,4]{1,0:T(2,128)S(1)} all-reduce(f32[2,4]{1,0:T(2,128)S(1)} %get-tuple-element.3), channel_id=1, replica_groups=mesh['dp'=8,'tensor'=16] {'tensor'}, use_global_device_ids=true, to_apply=%region_7.8 | all-reduce | flops 8 | bytes 64 | tf_op jit(solution)/shard_map/psum | solution.py:90
  202.8 19.9 %all-gather.1 = f32[8,2,4]{2,1,0:T(2,128)S(1)} all-gather(f32[1,2,4]{2,1,0:T(2,128)S(1)} %bitcast.102), channel_id=1, replica_groups=mesh['dp'=8,'tensor'=16] {'dp'}, dimensions={0}, use_global_device_ids=true | all-gather | bytes 288 | tf_op jit(solution)/shard_map/all_gather | solution.py:91
  222.7 0.6 broadcast_subtract_fusion
  223.3 4.0 %gather_fusion = bf16[8,256,256]{2,1,0:T(8,128)(2,1)S(1)} fusion(bf16[16,4,256,256]{3,2,1,0:T(8,128)(2,1)} %bitcast.100, s32[8]{0:T(128)S(1)} %reshape.166), kind=kCustom, calls=%fused_computation | custom fusion | bytes 2097216 | tf_op jit(solution)/shard_map/gather | solution.py:102
  227.3 1.1 broadcast_select_fusion
  (39 shorter events, 0.9 us)
Async XLA Ops:
  7.2 52.3 %all-gather.5.cloned.1.call-start = ((), (), s32[]{:S(2)}) async-start(), calls=%async_computation.1 | async-start | bytes 4718592 | tf_op jit(solution)/shard_map/all_gather | solution.py:60
  7.9 161.9 %reduce-scatter.4.cloned.1.call-start = ((), (), s32[]{:S(2)}) async-start(), calls=%async_computation.3 | async-start | bytes 4456448
  53.8 4.8 %copy-start = (bf16[2,4,256,1,256]{4,2,3,1,0:T(8,128)(2,1)S(1)}, bf16[2,4,256,1,256]{4,2,3,1,0:T(8,128)(2,1)}, u32[]{:S(2)}) copy-start(bf16[2,4,256,1,256]{4,2,3,1,0:T(8,128)(2,1)} %param.20) | copy-start | bytes 3145732
  53.8 5.5 %copy-start.4 = (s32[4]{0:T(128)S(1)}, s32[4]{0:T(128)}, u32[]{:S(2)}) copy-start(s32[4]{0:T(128)} %param.19) | copy-start | bytes 52
  85.9 1.3 copy-start.2
  85.9 85.4 %copy-start.1 = (bf16[2,4,512]{2,1,0:T(4,128)(2,1)S(1)}, bf16[2,4,512]{2,1,0:T(4,128)(2,1)}, u32[]{:S(2)}) copy-start(bf16[2,4,512]{2,1,0:T(4,128)(2,1)} %param.13) | copy-start | bytes 24580
  85.9 116.9 %copy-start.3 = (f32[2,4]{1,0:T(2,128)S(1)}, f32[2,4]{1,0:T(2,128)}, u32[]{:S(2)}) copy-start(f32[2,4]{1,0:T(2,128)} %param.22) | copy-start | bytes 100
  85.9 137.4 %all-gather.7.cloned.1.call-start = ((), (), s32[]{:S(2)}) async-start(), calls=%async_computation.2 | async-start | bytes 9437184 | tf_op jit(solution)/shard_map/all_gather | solution.py:99
Sparse Core Ops, SparseCore 0:
  9.7 35.6 all-gather.4
  86.1 83.7 reduce-scatter.3
  172.2 50.9 all-gather.6
where the time goes:
time: 236 us; the launch traced here: 235 us
  blocking collectives  90.4 us (38%)
  waiting for transfers between devices  82.9 us (35%)
  local copies, waits for them, and re-layouts  23.3 us (10%)
  matrix products  17.1 us (7%)
  between operations  13.9 us (6%)
  other arithmetic  7.24 us (3%)
    unnamed x4, waiting for transfers between devices  82.9 us
    psum x1, blocking collectives, per_device(): updated = log_weight + lax.psum(partial_dot, 'tensor')  30.9 us
    all_gather x1, blocking collectives, per_device(): lax.all_gather(norm_gain, 'tensor', axis=0, tiled=True)  20.9 us
    all_gather x1, blocking collectives, per_device(): every_weight = lax.all_gather(updated, 'dp', axis=0, tiled=True)  19.9 us
    unnamed x15, local copies, waits for them, and re-layouts  18.8 us
    all_gather x1, blocking collectives, per_device(): lax.all_gather(stream, 'tensor', axis=2, tiled=True)  18.7 us
  transfers between devices with their start and end apart: 3, of which 1 were waited for; matrix products, arithmetic and copies ran while one was open for 7% of the time, Pallas kernels for 0%

commit v1 on v0

v1 whole, which is shorter than its diff:
```python
import functools

import jax
import jax.numpy as jnp
from jax import lax
from jax.experimental import pallas as pl
from jax.experimental.pallas import tpu as pltpu
from jax.sharding import PartitionSpec as P

MESH = pl.DeviceIdType.MESH
F32 = jnp.float32
BF16 = jnp.bfloat16
LOW = -1e30


def dot(a, b):
    return jnp.dot(a, b, preferred_element_type=F32)


def dot_t(a, b):
    return lax.dot_general(a, b, (((1,), (1,)), ((), ())), preferred_element_type=F32)


def step_kernel(
    n_dp,
    n_t,
    stream_ref,
    gain_ref,
    pot_ref,
    wq_hbm,
    wkv_hbm,
    wo_hbm,
    pre_hbm,
    suf_hbm,
    plen_ref,
    slen_ref,
    lw_ref,
    group_ref,
    member_ref,
    mixed_ref,
    norm_ref,
    new_hbm,
    wq,
    wkv,
    wo,
    pre,
    suf,
    block_out,
    block_in,
    new,
    x_out,
    x_in,
    qkv_out,
    qkv_in,
    att_out,
    att_in,
    proj_out,
    proj_in,
    part_out,
    part_in,
    upd_out,
    upd_in,
    local_sem,
    new_sem,
    block_ssem,
    block_rsem,
    x_ssem,
    x_rsem,
    qkv_ssem,
    qkv_rsem,
    att_ssem,
    att_rsem,
    proj_ssem,
    proj_rsem,
    part_ssem,
    part_rsem,
    upd_ssem,
    upd_rsem,
):
    me = lax.axis_index("dp")
    mt = lax.axis_index("tensor")

    def dp_peer(k):
        return lax.rem(me + k, n_dp)

    def t_peer(k):
        return lax.rem(mt + k, n_t)

    def to_dp(src, dst, ssem, rsem, k):
        return pltpu.make_async_remote_copy(
            src_ref=src, dst_ref=dst, send_sem=ssem, recv_sem=rsem,
            device_id=(dp_peer(k), mt), device_id_type=MESH,
        )

    def to_t(src, dst, ssem, rsem, k):
        return pltpu.make_async_remote_copy(
            src_ref=src, dst_ref=dst, send_sem=ssem, recv_sem=rsem,
            device_id=(me, t_peer(k)), device_id_type=MESH,
        )

    def each(n, body):
        def run(k, carry):
            body(k)
            return carry

        lax.fori_loop(1, n, run, 0)

    load_suf = pltpu.make_async_copy(suf_hbm, suf, local_sem.at[0])
    load_wq = pltpu.make_async_copy(wq_hbm, wq, local_sem.at[1])
    load_wkv = pltpu.make_async_copy(wkv_hbm, wkv, local_sem.at[2])
    load_pre = pltpu.make_async_copy(pre_hbm, pre, local_sem.at[3])
    load_suf.start()
    load_wq.start()
    load_wkv.start()
    load_pre.start()
    width = wo.shape[2]
    load_wo = [
        pltpu.make_async_copy(
            wo_hbm.at[:, pl.ds(c * width, width)], wo.at[c], local_sem.at[4 + c]
        )
        for c in range(n_t)
    ]
    for c in range(n_t):
        load_wo[c].start()

    barrier = pltpu.get_barrier_semaphore()
    each(n_t, lambda k: pl.semaphore_signal(
        barrier, inc=1, device_id=(me, t_peer(k)), device_id_type=MESH))
    each(n_dp, lambda k: pl.semaphore_signal(
        barrier, inc=1, device_id=(dp_peer(k), mt), device_id_type=MESH))
    pl.semaphore_wait(barrier, n_t + n_dp - 2)

    x0 = stream_ref[0].astype(F32)
    x1 = stream_ref[1].astype(F32)
    x_own = jnp.concatenate([x0, x1], axis=0)
    half = width // 2
    gain_row = gain_ref[...].astype(F32).reshape(1, width)
    pot_row = pot_ref[...].astype(F32).reshape(1, width)
    rows = [gain_row[:, c * 128:(c + 1) * 128] for c in range(4)]
    rows += [pot_row[:, c * 128:(c + 1) * 128] for c in range(4)]
    vectors = jnp.concatenate(rows, axis=0)
    x_out[:, :half] = jnp.concatenate([x_own[:, :half], x_own[:, half:]], axis=0).astype(BF16)
    x_out[:, half:] = jnp.concatenate([vectors, vectors], axis=0).astype(BF16)

    def send_x(k):
        to_t(x_out, x_in.at[mt], x_ssem.at[k - 1], x_rsem.at[k - 1], k).start()

    each(n_t, send_x)
    x_in[mt] = x_out[...]

    load_suf.wait()

    def choose(j):
        first = jnp.int32(0)
        second = jnp.int32(0)
        count = jnp.int32(0)
        for p in range(2):
            for q in range(4):
                hit = group_ref[q, 2 * j + p] == me
                at = member_ref[q, 2 * j + p] * 4 + q
                first = jnp.where(hit & (count == 0), at, first)
                second = jnp.where(hit & (count == 1), at, second)
                count = count + hit.astype(jnp.int32)
        return first, second

    def send_blocks(k):
        first, second = choose(dp_peer(k))
        block_out[k - 1, 0] = suf[first]
        block_out[k - 1, 1] = suf[second]
        to_dp(block_out.at[k - 1], block_in.at[me], block_ssem.at[k - 1], block_rsem.at[k - 1], k).start()

    each(n_dp, send_blocks)
    first, second = choose(me)
    block_in[me, 0] = suf[first]
    block_in[me, 1] = suf[second]

    lane512 = lax.broadcasted_iota(jnp.int32, (8, 512), 1)
    spread_r = lax.broadcasted_iota(jnp.int32, (128, 512), 0)
    spread_c = lax.broadcasted_iota(jnp.int32, (128, 512), 1)
    spread = jnp.where(spread_c // 4 == spread_r, 1.0, 0.0).astype(BF16)

    def wait_x(k):
        to_t(x_out, x_in.at[t_peer(n_t - k)], x_ssem.at[k - 1], x_rsem.at[k - 1], k).wait_recv()

    each(n_t, wait_x)
    squares = jnp.zeros((16, half), F32)
    for c in range(n_t):
        part = x_in[c, :, :half].astype(F32)
        squares = squares + part * part
    squares = squares[:8] + squares[8:]
    scale = lax.rsqrt(jnp.sum(squares, axis=1, keepdims=True) * (1.0 / (width * n_t)) + 1e-05)
    load_wkv.wait()
    load_wq.wait()
    q_acc = jnp.zeros((32, 128), F32)
    kv_acc = jnp.zeros((8, 256), F32)
    for c in range(n_t):
        part = x_in[c, :, :half].astype(F32)
        part = jnp.concatenate([part[:8], part[8:]], axis=1)
        gains = x_in[c, :, half:].astype(F32)
        gain = jnp.concatenate([gains[r:r + 1] for r in range(4)], axis=1)
        normed = (part * scale * gain).astype(BF16)
        kv_acc = kv_acc + dot(normed, wkv[c * width:(c + 1) * width, :])
        for b in range(4):
            wide = dot(normed[:, b * 128:(b + 1) * 128], spread)
            lhs = jnp.concatenate(
                [jnp.where(lane512 % 4 == h, wide, 0.0) for h in range(4)], axis=0
            ).astype(BF16)
            start = (c * 4 + b) * 512
            q_acc = q_acc + dot(lhs, wq[start:start + 512, :])

    row = lax.broadcasted_iota(jnp.int32, (32, 32), 0)
    col = lax.broadcasted_iota(jnp.int32, (32, 32), 1)
    source = (row % 4) * 8 + ((row // 4) % 2) * 4 + row // 8
    turn = jnp.where(col == source, 1.0, 0.0).astype(BF16)
    q_rows = dot(turn, (q_acc * (128 ** -0.5)).astype(BF16))
    qkv_out[0:32, :] = q_rows.astype(BF16)
    qkv_out[32:48, :] = jnp.concatenate([kv_acc[:, :128], kv_acc[:, 128:]], axis=0).astype(BF16)

    def send_qkv(k):
        to_dp(qkv_out, qkv_in.at[me], qkv_ssem.at[k - 1], qkv_rsem.at[k - 1], k).start()

    each(n_dp, send_qkv)
    qkv_in[me] = qkv_out[...]

    place = lax.broadcasted_iota(jnp.int32, (256, 1), 0)
    place_row = lax.broadcasted_iota(jnp.int32, (8, 256), 1)
    second_half = lax.broadcasted_iota(jnp.int32, (8, 1), 0) >= 4
    fresh = qkv_out[32:48, :].astype(F32)
    suf_top, suf_total, suf_att = [], [], []
    for q in range(4):
        q_tile = q_rows[q * 8:(q + 1) * 8].astype(BF16)
        scores, values = [], []
        for p in range(2):
            tok = p * 4 + q
            length = slen_ref[q, 2 * me + p]
            keys = suf[tok, :, :128].astype(F32)
            vals = suf[tok, :, 128:].astype(F32)
            keys = jnp.where(place == length, fresh[tok:tok + 1], keys).astype(BF16)
            vals = jnp.where(place == length, fresh[8 + tok:9 + tok], vals).astype(BF16)
            s = dot_t(q_tile, keys)
            scores.append(jnp.where(place_row <= length, s, LOW))
            values.append(vals)
        s = jnp.where(second_half, scores[1], scores[0])
        top = jnp.max(s, axis=1, keepdims=True)
        e = jnp.exp(s - top)
        suf_top.append(top)
        suf_total.append(jnp.sum(e, axis=1, keepdims=True))
        e16 = e.astype(BF16)
        suf_att.append(jnp.where(second_half, dot(e16, values[1]), dot(e16, values[0])))

    for c in range(n_t):
        load_wo[c].wait()
    probe = jnp.zeros((8, width), F32)
    for c in range(n_t):
        vec = x_in[c, :, half:].astype(F32)
        pots = jnp.concatenate([vec[4 + r:5 + r] for r in range(4)], axis=1)
        pots = jnp.broadcast_to(pots, (8, width)).astype(BF16)
        probe = probe + dot_t(pots, wo[c])

    load_pre.wait()

    def wait_qkv(k):
        to_dp(qkv_out, qkv_in.at[dp_peer(n_dp - k)], qkv_ssem.at[k - 1], qkv_rsem.at[k - 1], k).wait_recv()

    each(n_dp, wait_qkv)
    lane8 = lax.broadcasted_iota(jnp.int32, (64, 128), 1)
    q_all = [qkv_in[j, 0:32, :].astype(F32) for j in range(n_dp)]
    place_pre = lax.broadcasted_iota(jnp.int32, (64, 256), 1) + me * 256
    stats = jnp.zeros((64, 128), F32)
    for q in range(4):
        q_mat = jnp.concatenate([q_all[j][q * 8:(q + 1) * 8] for j in range(n_dp)], axis=0).astype(BF16)
        valid = place_pre < plen_ref[q]
        s = jnp.where(valid, dot_t(q_mat, pre[q, :, :128]), LOW)
        top = jnp.max(s, axis=1, keepdims=True)
        e = jnp.where(valid, jnp.exp(s - top), 0.0)
        total = jnp.sum(e, axis=1, keepdims=True)
        o = dot(e.astype(BF16), pre[q, :, 128:])
        for j in range(n_dp):
            att_out[j, q * 8:(q + 1) * 8, :] = o[j * 8:(j + 1) * 8]
        stats = jnp.where(lane8 == q, top, stats)
        stats = jnp.where(lane8 == 4 + q, total, stats)
    for j in range(n_dp):
        att_out[j, 32:40, :] = stats[j * 8:(j + 1) * 8]

    def send_att(k):
        j = dp_peer(k)
        to_dp(att_out.at[j], att_in.at[me], att_ssem.at[k - 1], att_rsem.at[k - 1], k).start()

    each(n_dp, send_att)
    att_in[me] = att_out[me]

    def wait_att(k):
        to_dp(att_out.at[dp_peer(k)], att_in.at[dp_peer(n_dp - k)], att_ssem.at[k - 1], att_rsem.at[k - 1], k).wait_recv()

    each(n_dp, wait_att)

    lane = lax.broadcasted_iota(jnp.int32, (8, 128), 1)
    all_stats = [att_in[j, 32:40, :] for j in range(n_dp)]
    attended = []
    for q in range(4):
        tops = [st[:, q:q + 1] for st in all_stats]
        totals = [st[:, 4 + q:5 + q] for st in all_stats]
        best = suf_top[q]
        for j in range(n_dp):
            best = jnp.maximum(best, tops[j])
        factor = jnp.exp(suf_top[q] - best)
        denom = factor * suf_total[q]
        numer = factor * suf_att[q]
        for j in range(n_dp):
            factor = jnp.exp(tops[j] - best)
            denom = denom + factor * totals[j]
            numer = numer + factor * att_in[j, q * 8:(q + 1) * 8, :]
        attended.append(numer / denom)
    att_rows = jnp.concatenate(attended, axis=0).astype(BF16)
    by_head = dot(turn, att_rows)
    att_lhs = jnp.concatenate([by_head[h * 8:(h + 1) * 8] for h in range(4)], axis=1)

    part = jnp.sum(att_lhs * probe + x_own * pot_row, axis=1, keepdims=True)
    part_out[...] = jnp.broadcast_to(part, (8, 128))

    def send_part(k):
        to_t(part_out, part_in.at[mt], part_ssem.at[k - 1], part_rsem.at[k - 1], k).start()

    each(n_t, send_part)
    part_in[mt] = part_out[...]

    lhs = att_lhs.astype(BF16)

    def send_proj(k):
        t = t_peer(k)
        proj_out[k - 1] = dot(lhs, wo[t])
        to_t(proj_out.at[k - 1], proj_in.at[mt], proj_ssem.at[k - 1], proj_rsem.at[k - 1], k).start()

    each(n_t, send_proj)
    shared = dot(lhs, wo[mt])
    proj_in[mt] = shared

    def wait_part(k):
        to_t(part_out, part_in.at[t_peer(n_t - k)], part_ssem.at[k - 1], part_rsem.at[k - 1], k).wait_recv()

    each(n_t, wait_part)
    inner = part_in[0]
    for c in range(1, n_t):
        inner = inner + part_in[c]
    sub = lax.broadcasted_iota(jnp.int32, (8, 128), 0)
    weight = jnp.zeros((8, 128), F32)
    for p in range(2):
        for q in range(4):
            weight = jnp.where(sub == p * 4 + q, lw_ref[p, q], weight)
    updated = weight + inner
    upd_out[...] = updated

    def send_upd(k):
        to_dp(upd_out, upd_in.at[me], upd_ssem.at[k - 1], upd_rsem.at[k - 1], k).start()

    each(n_dp, send_upd)
    upd_in[me] = updated

    def wait_blocks(k):
        to_dp(block_out.at[k - 1], block_in.at[dp_peer(n_dp - k)], block_ssem.at[k - 1], block_rsem.at[k - 1], k).wait_recv()

    each(n_dp, wait_blocks)
    row16 = lax.broadcasted_iota(jnp.int32, (16, 128), 0)
    named = []
    for p in range(2):
        for q in range(4):
            tok = p * 4 + q
            g = group_ref[q, 2 * me + p]
            m = member_ref[q, 2 * me + p]
            slot = jnp.int32(0)
            for other in named:
                slot = slot + (other == g).astype(jnp.int32)
            named.append(g)
            length = slen_ref[q, 2 * g + m]
            line = qkv_in[g, 32:48, :].astype(F32)
            line_k = jnp.sum(jnp.where(row16 == m * 4 + q, line, 0.0), axis=0, keepdims=True)
            line_v = jnp.sum(jnp.where(row16 == 8 + m * 4 + q, line, 0.0), axis=0, keepdims=True)
            line = jnp.concatenate([line_k, line_v], axis=1)
            block = block_in[g, jnp.minimum(slot, 1)].astype(F32)
            new[tok] = jnp.where(place == length, line, block).astype(BF16)
            pltpu.make_async_copy(new.at[tok], new_hbm.at[tok], new_sem.at[tok]).start()

    def wait_proj(k):
        to_t(proj_out.at[k - 1], proj_in.at[t_peer(n_t - k)], proj_ssem.at[k - 1], proj_rsem.at[k - 1], k).wait_recv()

    each(n_t, wait_proj)
    shared = proj_in[0]
    for c in range(1, n_t):
        shared = shared + proj_in[c]
    mixed = x_own + shared
    mixed_ref[0] = mixed[:4].astype(BF16)
    mixed_ref[1] = mixed[4:].astype(BF16)

    def wait_upd(k):
        to_dp(upd_out, upd_in.at[dp_peer(n_dp - k)], upd_ssem.at[k - 1], upd_rsem.at[k - 1], k).wait_recv()

    each(n_dp, wait_upd)
    everyone = [upd_in[j] for j in range(n_dp)]
    best = everyone[0]
    for j in range(1, n_dp):
        best = jnp.maximum(best, everyone[j])
    best = jnp.maximum(best, jnp.concatenate([best[4:], best[:4]], axis=0))
    total = jnp.zeros((8, 128), F32)
    for j in range(n_dp):
        total = total + jnp.exp(everyone[j] - best)
    total = total + jnp.concatenate([total[4:], total[:4]], axis=0)
    normalized = updated - (best + jnp.log(total))
    picked = jnp.where(sub % 4 == lane, normalized, 0.0)
    norm_ref[...] = jnp.concatenate(
        [jnp.sum(picked[:4], axis=0, keepdims=True), jnp.sum(picked[4:], axis=0, keepdims=True)], axis=0
    )[:, :4]

    for tok in range(8):
        pltpu.make_async_copy(new.at[tok], new_hbm.at[tok], new_sem.at[tok]).wait()

    def done_dp(k):
        to_dp(block_out.at[k - 1], block_in.at[me], block_ssem.at[k - 1], block_rsem.at[k - 1], k).wait_send()
        to_dp(qkv_out, qkv_in.at[me], qkv_ssem.at[k - 1], qkv_rsem.at[k - 1], k).wait_send()
        to_dp(att_out.at[dp_peer(k)], att_in.at[me], att_ssem.at[k - 1], att_rsem.at[k - 1], k).wait_send()
        to_dp(upd_out, upd_in.at[me], upd_ssem.at[k - 1], upd_rsem.at[k - 1], k).wait_send()

    def done_t(k):
        to_t(x_out, x_in.at[mt], x_ssem.at[k - 1], x_rsem.at[k - 1], k).wait_send()
        to_t(part_out, part_in.at[mt], part_ssem.at[k - 1], part_rsem.at[k - 1], k).wait_send()
        to_t(proj_out.at[k - 1], proj_in.at[mt], proj_ssem.at[k - 1], proj_rsem.at[k - 1], k).wait_send()

    each(n_dp, done_dp)
    each(n_t, done_t)


def per_device(
    n_dp,
    n_t,
    stream,
    norm_gain,
    w_q,
    w_kv,
    w_o,
    prefix_kv,
    prompt_len,
    suffix_kv,
    suffix_len,
    log_weight,
    potential,
    anc_group,
    anc_member,
):
    vmem = pl.BlockSpec(memory_space=pltpu.VMEM)
    smem = pl.BlockSpec(memory_space=pltpu.SMEM)
    hbm = pl.BlockSpec(memory_space=pl.ANY)
    dma = pltpu.SemaphoreType.DMA
    mixed, normalized, new = pl.pallas_call(
        functools.partial(step_kernel, n_dp, n_t),
        out_shape=(
            jax.ShapeDtypeStruct((2, 4, 512), BF16),
            jax.ShapeDtypeStruct((2, 4), F32),
            jax.ShapeDtypeStruct((8, 256, 256), BF16),
        ),
        in_specs=[vmem, vmem, vmem, hbm, hbm, hbm, hbm, hbm, smem, smem, smem, smem, smem],
        out_specs=(vmem, vmem, hbm),
        scratch_shapes=[
            pltpu.VMEM((32768, 128), BF16),
            pltpu.VMEM((8192, 256), BF16),
            pltpu.VMEM((n_t, 512, 512), BF16),
            pltpu.VMEM((4, 256, 256), BF16),
            pltpu.VMEM((8, 256, 256), BF16),
            pltpu.VMEM((n_dp - 1, 2, 256, 256), BF16),
            pltpu.VMEM((n_dp, 2, 256, 256), BF16),
            pltpu.VMEM((8, 256, 256), BF16),
            pltpu.VMEM((16, 384), BF16),
            pltpu.VMEM((n_t, 16, 384), BF16),
            pltpu.VMEM((48, 128), BF16),
            pltpu.VMEM((n_dp, 48, 128), BF16),
            pltpu.VMEM((n_dp, 40, 128), F32),
            pltpu.VMEM((n_dp, 40, 128), F32),
            pltpu.VMEM((n_t - 1, 8, 512), F32),
            pltpu.VMEM((n_t, 8, 512), F32),
            pltpu.VMEM((8, 128), F32),
            pltpu.VMEM((n_t, 8, 128), F32),
            pltpu.VMEM((8, 128), F32),
            pltpu.VMEM((n_dp, 8, 128), F32),
            dma((4 + n_t,)),
            dma((8,)),
            dma((n_dp - 1,)),
            dma((n_dp - 1,)),
            dma((n_t - 1,)),
            dma((n_t - 1,)),
            dma((n_dp - 1,)),
            dma((n_dp - 1,)),
            dma((n_dp - 1,)),
            dma((n_dp - 1,)),
            dma((n_t - 1,)),
            dma((n_t - 1,)),
            dma((n_t - 1,)),
            dma((n_t - 1,)),
            dma((n_dp - 1,)),
            dma((n_dp - 1,)),
        ],
        compiler_params=pltpu.CompilerParams(
            collective_id=0, has_side_effects=True, vmem_limit_bytes=48 * 1024 * 1024
        ),
    )(
        stream,
        norm_gain,
        potential,
        w_q.reshape(32768, 128),
        w_kv.reshape(8192, 256),
        w_o.reshape(512, 8192),
        prefix_kv.reshape(4, 256, 256),
        suffix_kv.reshape(8, 256, 256),
        prompt_len,
        suffix_len.T,
        log_weight,
        anc_group[:, :, 0].T,
        anc_member.T,
    )
    return mixed, normalized, new.reshape(2, 4, 256, 1, 256)


def solution(mesh):
    placed = (
        P("dp", None, "tensor"),
        P("tensor"),
        P(None, "tensor", None),
        P(None, "tensor", None),
        P("tensor", None, None),
        P(None, "dp", "tensor", None),
        P(),
        P("dp", None, None, "tensor", None),
        P(),
        P("dp", None),
        P("tensor"),
        P(),
        P(),
    )
    return jax.shard_map(
        functools.partial(per_device, mesh.shape["dp"], mesh.shape["tensor"]),
        mesh=mesh,
        in_specs=placed,
        out_specs=(P("dp", None, "tensor"), P("dp", None), P("dp", None, None, "tensor", None)),
        check_vma=False,
    )
```

time: 236 us -> 62 us (0.26)
  blocking collectives: 90.4 us -> 0 us
  waiting for transfers between devices: 82.9 us -> 0 us
  Pallas kernels: 0 us -> 51.1 us
  matrix products: 17.1 us -> 0 us
  local copies, waits for them, and re-layouts: 23.3 us -> 9.82 us
  between operations: 13.9 us -> 0.66 us
  other arithmetic: 7.24 us -> 0 us
    unnamed x4 -> x0, waiting for transfers between devices: 82.9 us -> none
    all_gather x3 -> x0, blocking collectives: 59.5 us -> none  [the longest x1 20.9 us: per_device(): lax.all_gather(norm_gain, 'tensor', axis=0, tiled=True)]
    pallas_call x0 -> x1, Pallas kernels: none -> 51.1 us  [per_device(): pl.pallas_call(functools.partial(step_kernel, n_dp, n_t), out_shape=(jax....]
    psum x1 -> x0, blocking collectives: 30.9 us -> none  [per_device(): updated = log_weight + lax.psum(partial_dot, 'tensor')]
    dot_general x7 -> x0, matrix products: 17.1 us -> none  [the longest x1 4.67 us: per_device(): jnp.dot(normed, w_q.reshape(model_width, -1), preferred_element_type=jnp....]
    unnamed x15 -> x23, local copies, waits for them, and re-layouts: 18.8 us -> 9.82 us
    gather x1 -> x0, local copies, waits for them, and re-layouts: 4 us -> none  [per_device(): piece[jnp.clip(own_ancestor, 0, row_count - 1), prompt_index[None, :]]]
    select_n x3 -> x0, other arithmetic: 2.79 us -> none  [the longest x2 1.68 us: per_device(): jnp.where(landing[:, :, :, None, None], fresh[:, :, None], suffix_kv)]
  transfers between devices with their start and end apart: 3 -> 0, of which waited for: 1 -> 0; matrix products, arithmetic and copies ran while one was open for 7% -> 0% of each run, Pallas kernels for 0% -> 0%
where the time goes in v1:
time: 62 us; the launch traced here: 61.6 us
  Pallas kernels  51.1 us (82%)
  local copies, waits for them, and re-layouts  9.82 us (16%)
  between operations  0.66 us (1%)
    pallas_call x1, Pallas kernels, per_device(): pl.pallas_call(functools.partial(step_kernel, n_dp, n_t), out_shape=(jax....  51.1 us
    unnamed x23, local copies, waits for them, and re-layouts  9.82 us

profile of v1, /device:TPU:1, one launch (start us, length us, event | category | flops | bytes accessed | tf_op | source)
XLA Modules:
  0.0 61.6 jit_solution(3225413831439863744)
XLA Ops:
  0.6 0.0 copy-start
  0.6 1.2 %copy-done = bf16[2,4,256,1,256]{4,2,3,1,0:T(8,128)(2,1)S(1)} copy-done((bf16[2,4,256,1,256]{4,2,3,1,0:T(8,128)(2,1)S(1)}, bf16[2,4,256,1,256]{4,2,3,1,0:T(8,128)(2,1)}, u32[]{:S(2)}) %copy-start) | copy-done | bytes 1048600
  1.9 0.0 copy-start.1
  1.9 1.0 %copy-done.1 = bf16[4,256,1,256]{3,1,2,0:T(8,128)(2,1)S(1)} copy-done((bf16[4,256,1,256]{3,1,2,0:T(8,128)(2,1)S(1)}, bf16[4,256,1,256]{3,1,2,0:T(8,128)(2,1)}, u32[]{:S(2)}) %copy-start.1) | copy-done | bytes 524312
  2.9 0.0 copy-start.2
  2.9 0.7 %copy-done.2 = bf16[2,4,512]{2,1,0:T(4,128)(2,1)S(1)} copy-done((bf16[2,4,512]{2,1,0:T(4,128)(2,1)S(1)}, bf16[2,4,512]{2,1,0:T(4,128)(2,1)}, u32[]{:S(2)}) %copy-start.2) | copy-done | bytes 8216
  3.6 0.0 copy-start.3
  3.6 0.7 %copy-done.3 = s32[16,4]{0,1:T(4,128)S(1)} copy-done((s32[16,4]{0,1:T(4,128)S(1)}, s32[16,4]{0,1:T(4,128)}, u32[]{:S(2)}) %copy-start.3) | copy-done | bytes 280
  4.3 0.0 copy-start.4
  4.3 0.7 %copy-done.4 = s32[16,4,1]{0,2,1:T(1,128)S(1)} copy-done((s32[16,4,1]{0,2,1:T(1,128)S(1)}, s32[16,4,1]{0,2,1:T(1,128)}, u32[]{:S(2)}) %copy-start.4) | copy-done | bytes 280
  5.0 0.0 copy-start.5
  5.0 0.7 %copy-done.5 = s32[16,4]{0,1:T(4,128)S(1)} copy-done((s32[16,4]{0,1:T(4,128)S(1)}, s32[16,4]{0,1:T(4,128)}, u32[]{:S(2)}) %copy-start.5) | copy-done | bytes 280
  5.6 0.0 copy-start.6
  5.6 0.7 %copy-done.6 = bf16[512]{0:T(512)(128)(2,1)S(1)} copy-done((bf16[512]{0:T(512)(128)(2,1)S(1)}, bf16[512]{0:T(512)(128)(2,1)}, u32[]{:S(2)}) %copy-start.6) | copy-done | bytes 1048
  6.3 0.0 copy-start.7
  6.3 0.7 %copy-done.7 = bf16[512]{0:T(512)(128)(2,1)S(1)} copy-done((bf16[512]{0:T(512)(128)(2,1)S(1)}, bf16[512]{0:T(512)(128)(2,1)}, u32[]{:S(2)}) %copy-start.7) | copy-done | bytes 1048
  7.0 0.0 copy-start.8
  7.0 0.7 %copy-done.8 = f32[2,4]{1,0:T(2,128)S(1)} copy-done((f32[2,4]{1,0:T(2,128)S(1)}, f32[2,4]{1,0:T(2,128)}, u32[]{:S(2)}) %copy-start.8) | copy-done | bytes 56
  7.7 0.0 copy-start.9
  7.7 0.7 %copy-done.9 = s32[4]{0:T(128)S(1)} copy-done((s32[4]{0:T(128)S(1)}, s32[4]{0:T(128)}, u32[]{:S(2)}) %copy-start.9) | copy-done | bytes 40
  8.3 51.1 %shard_map.148 = (bf16[2,4,512]{2,1,0:T(4,128)(2,1)S(1)}, f32[2,4]{1,0:T(2,128)S(1)}, bf16[8,256,256]{2,1,0:T(8,128)(2,1)S(1)}) custom-call(bf16[2,4,512]{2,1,0:T(4,128)(2,1)S(1)} %copy-done.2, bf16[512]{0:T(512)(128)(2,1)S(1)} %copy-done.6, bf16[512]{0:T(512)(128)(2,1)S(1)} %copy-done.7, bf16[32768,128]{1,0:T(8,128)(2,1)} %bitcast.19, ...), custom_call_target="tpu_custom_call" | custom-call | tf_op jit(solution)/shard_map/pallas_call | solution.py:452
  59.5 0.6 copy.20
  60.1 0.6 copy.21
  60.6 1.0 %copy.22 = bf16[2,4,256,1,256]{4,2,3,1,0:T(8,128)(2,1)} copy(bf16[2,4,256,1,256]{4,2,3,1,0:T(8,128)(2,1)S(1)} %bitcast.14) | data formatting | bytes 2097152
Async XLA Ops:
  0.6 1.2 %copy-start = (bf16[2,4,256,1,256]{4,2,3,1,0:T(8,128)(2,1)S(1)}, bf16[2,4,256,1,256]{4,2,3,1,0:T(8,128)(2,1)}, u32[]{:S(2)}) copy-start(bf16[2,4,256,1,256]{4,2,3,1,0:T(8,128)(2,1)} %param.20) | copy-start | bytes 3145732
  1.9 1.0 %copy-start.1 = (bf16[4,256,1,256]{3,1,2,0:T(8,128)(2,1)S(1)}, bf16[4,256,1,256]{3,1,2,0:T(8,128)(2,1)}, u32[]{:S(2)}) copy-start(bf16[4,256,1,256]{3,1,2,0:T(8,128)(2,1)} %param.18) | copy-start | bytes 1572868
  2.9 0.7 %copy-start.2 = (bf16[2,4,512]{2,1,0:T(4,128)(2,1)S(1)}, bf16[2,4,512]{2,1,0:T(4,128)(2,1)}, u32[]{:S(2)}) copy-start(bf16[2,4,512]{2,1,0:T(4,128)(2,1)} %stream_ref.1) | copy-start | bytes 24580
  3.6 0.7 %copy-start.3 = (s32[16,4]{0,1:T(4,128)S(1)}, s32[16,4]{0,1:T(4,128)}, u32[]{:S(2)}) copy-start(s32[16,4]{0,1:T(4,128)} %param.21) | copy-start | bytes 772
  4.3 0.7 %copy-start.4 = (s32[16,4,1]{0,2,1:T(1,128)S(1)}, s32[16,4,1]{0,2,1:T(1,128)}, u32[]{:S(2)}) copy-start(s32[16,4,1]{0,2,1:T(1,128)} %param.24) | copy-start | bytes 772
  5.0 0.7 %copy-start.5 = (s32[16,4]{0,1:T(4,128)S(1)}, s32[16,4]{0,1:T(4,128)}, u32[]{:S(2)}) copy-start(s32[16,4]{0,1:T(4,128)} %param.25) | copy-start | bytes 772
  5.6 0.7 %copy-start.6 = (bf16[512]{0:T(512)(128)(2,1)S(1)}, bf16[512]{0:T(512)(128)(2,1)}, u32[]{:S(2)}) copy-start(bf16[512]{0:T(512)(128)(2,1)} %gain_ref.1) | copy-start | bytes 3076
  6.3 0.7 %copy-start.7 = (bf16[512]{0:T(512)(128)(2,1)S(1)}, bf16[512]{0:T(512)(128)(2,1)}, u32[]{:S(2)}) copy-start(bf16[512]{0:T(512)(128)(2,1)} %pot_ref.1) | copy-start | bytes 3076
  7.0 0.7 %copy-start.8 = (f32[2,4]{1,0:T(2,128)S(1)}, f32[2,4]{1,0:T(2,128)}, u32[]{:S(2)}) copy-start(f32[2,4]{1,0:T(2,128)} %lw_ref.1) | copy-start | bytes 100
  7.7 0.7 %copy-start.9 = (s32[4]{0:T(128)S(1)}, s32[4]{0:T(128)}, u32[]{:S(2)}) copy-start(s32[4]{0:T(128)} %plen_ref.1) | copy-start | bytes 52
